TPU v7x, 512 devices: a whole 4x8x8 slice. The times are simulated.
512 devices in a mesh: pipe: 4 (over x), tm: 32 (over y_lo, z), dp: 4 (over y_hi, core).
Axes of the slice: x: 4, y: 8 (y_hi: 2, y_lo: 4; y = y_hi * 4 + y_lo), z: 8, core: 2. Of those that a mesh axis runs over, the one named last changes fastest.
Arguments:
- video: bfloat16 [4, 4, 64, 64, 320], P(None, 'dp', 'tm'), may hold values from -6 to 6
- cotangent: bfloat16 [4, 4, 64, 64, 320], P(None, 'dp', 'tm'), may hold values from -6 to 6
- timesteps: int32 [4, 4], P(None, 'dp'), may hold values from 0 to 999
- conv_weight: bfloat16 [4, 3, 320, 320], P('pipe'), may hold values from -0.1875 to 0.1875
- out_weight: bfloat16 [4, 320, 320], P('pipe'), may hold values from -0.3125 to 0.3125
Outputs:
- conv_grad: float32 [4, 3, 320, 320], P('pipe')
- out_grad: float32 [4, 320, 320], P('pipe')
All inputs are finite; a program needn't handle non-finite values.
Results may differ from a plain program's by a relative error of at most 0.012.
Values may be sent and summed in bfloat16 or wider, within the bound.
A program may use at most 64 MiB of HBM per device.

v0:
```python
import math
import jax
import jax.numpy as jnp
from jax import lax
from jax.sharding import PartitionSpec as P

EPSILON = 1e-06


def padded_2(block, sides, width):
    for axis, dim in sides:
        count = lax.axis_size(axis)
        forward = [(i, i + 1) for i in range(count - 1)]
        backward = [(target, source) for source, target in forward]
        low = lax.ppermute(
            lax.slice_in_dim(block, block.shape[dim] - width, None, axis=dim), axis, forward
        )
        high = lax.ppermute(lax.slice_in_dim(block, 0, width, axis=dim), axis, backward)
        block = jnp.concatenate([low, block, high], axis=dim)
    return block


def from_partner(value, axis, stride):
    mask = 2**stride
    pairs = [(source, source ^ mask) for source in range(lax.axis_size(axis))]
    return lax.ppermute(value, axis, pairs)


def from_behind(array, axis, by):
    peers = lax.axis_size(axis)
    pairs = [(i, i + by) for i in range(peers) if 0 <= i + by < peers]
    return lax.ppermute(array, axis, pairs)


def embed(times, channels):
    half = channels // 2
    index = jnp.arange(half).astype(jnp.float32)
    freq = jnp.exp(index * (-math.log(10000.0) / half))
    angle = times.astype(jnp.float32)[..., None] * freq
    return jnp.concatenate([jnp.sin(angle), jnp.cos(angle)], -1)


def prepare(inputs, emb_pair, conv_pair):
    x_float = inputs.astype(jnp.float32)
    inv_rms = lax.rsqrt(jnp.mean(x_float * x_float, -1, keepdims=True) + EPSILON)
    normed = x_float * inv_rms
    norm_low = normed.astype(jnp.bfloat16)
    padded = padded_2(norm_low, (("tm", 1),), 1)
    frames = inputs.shape[1]
    pre_act = emb_pair[:, None, None, :]
    for offset in range(3):
        pre_act = pre_act + jnp.einsum(
            "dfpc,dcx->dfpx",
            padded[:, offset : offset + frames],
            conv_pair[:, offset],
            preferred_element_type=jnp.float32,
        )
    active = jax.nn.silu(pre_act).astype(jnp.bfloat16)
    return (inv_rms, normed, padded, pre_act, active)


def body(video, cotangent, timesteps, conv_weight, out_weight):
    current_section_index = lax.axis_index("pipe")
    sections = lax.axis_size("pipe")
    final_section = sections - 1
    micro = video.shape[0]
    half_microbatch_count = micro // 2
    ticks = half_microbatch_count + sections - 1
    channels = video.shape[-1]
    frames = video.shape[2]
    bit_count = sections.bit_length() - 1
    packed = jnp.concatenate([conv_weight[0], out_weight[0][None]], 0)
    mirrored = packed
    for bit_pos in range(bit_count):
        mirrored = from_partner(mirrored, "pipe", bit_pos)
    conv_pair = jnp.stack([conv_weight[0], mirrored[:3]])
    out_pair = jnp.stack([out_weight[0], mirrored[3]])
    embedded = embed(timesteps[:, 0], channels)

    def pick(stacked, down_tick, up_tick):
        down_part = lax.dynamic_index_in_dim(
            stacked, jnp.clip(down_tick, 0, ticks - 1), 0, keepdims=False
        )[0]
        up_part = lax.dynamic_index_in_dim(
            stacked, jnp.clip(up_tick, 0, ticks - 1), 0, keepdims=False
        )[1]
        return jnp.stack([down_part, up_part])

    empty_activation = jnp.zeros(video.shape[2:], jnp.bfloat16)
    down_buf = empty_activation
    up_buf = empty_activation
    saved = []
    for current_clock_tick in range(ticks):
        down_in = down_buf
        up_in = up_buf
        if current_clock_tick < half_microbatch_count:
            down_in = jnp.where(current_section_index == 0, video[current_clock_tick, 0], down_buf)
            up_in = jnp.where(
                current_section_index == final_section,
                video[half_microbatch_count + current_clock_tick, 0],
                up_buf,
            )
        inputs = jnp.stack([down_in, up_in])
        down_row = lax.dynamic_index_in_dim(
            embedded,
            jnp.clip(current_clock_tick - current_section_index, 0, half_microbatch_count - 1),
            0,
            keepdims=False,
        )
        up_row = lax.dynamic_index_in_dim(
            embedded,
            half_microbatch_count
            + jnp.clip(
                current_clock_tick - (final_section - current_section_index),
                0,
                half_microbatch_count - 1,
            ),
            0,
            keepdims=False,
        )
        emb_pair = jnp.stack([down_row, up_row])
        inv_rms, normed, padded, pre_act, active = prepare(inputs, emb_pair, conv_pair)
        outputs = (
            inputs.astype(jnp.float32)
            + jnp.einsum("dfpc,dcx->dfpx", active, out_pair, preferred_element_type=jnp.float32)
        ).astype(jnp.bfloat16)
        saved.append((inv_rms, normed, padded, pre_act, active))
        if current_clock_tick + 1 < ticks:
            down_buf = from_behind(outputs[0], "pipe", 1)
            up_buf = from_behind(outputs[1], "pipe", -1)
    stored = jax.tree.map(lambda *leaves: jnp.stack(leaves), *saved)
    conv_acc = jnp.zeros((2, 3, channels, channels), jnp.float32)
    out_acc = jnp.zeros((2, channels, channels), jnp.float32)
    downward_gradient_holder = empty_activation
    upward_gradient_holder = empty_activation
    for current_clock_tick in range(ticks):
        down_micro = current_clock_tick - (final_section - current_section_index)
        up_micro = current_clock_tick - current_section_index
        down_valid = (down_micro >= 0) & (down_micro < half_microbatch_count)
        up_valid = (up_micro >= 0) & (up_micro < half_microbatch_count)
        downward_hidden_gradient = downward_gradient_holder
        upward_hidden_gradient = upward_gradient_holder
        if current_clock_tick < half_microbatch_count:
            downward_hidden_gradient = jnp.where(
                current_section_index == final_section,
                cotangent[current_clock_tick, 0],
                downward_gradient_holder,
            )
            upward_hidden_gradient = jnp.where(
                current_section_index == 0,
                cotangent[half_microbatch_count + current_clock_tick, 0],
                upward_gradient_holder,
            )
        downward_hidden_gradient = jnp.where(down_valid, downward_hidden_gradient, empty_activation)
        upward_hidden_gradient = jnp.where(up_valid, upward_hidden_gradient, empty_activation)
        grad_out = jnp.stack([downward_hidden_gradient, upward_hidden_gradient])
        down_tick = down_micro + current_section_index
        up_tick = up_micro + final_section - current_section_index
        inv_rms, normed, padded, pre_act, active = tuple(
            (pick(item, down_tick, up_tick) for item in stored)
        )
        out_acc = out_acc + jnp.einsum(
            "dfpc,dfpx->dcx", active, grad_out, preferred_element_type=jnp.float32
        )
        grad_act = jnp.einsum(
            "dfpx,dcx->dfpc", grad_out, out_pair, preferred_element_type=jnp.float32
        )
        sigma = jax.nn.sigmoid(pre_act)
        grad_pre = (grad_act * sigma * (1.0 + pre_act * (1.0 - sigma))).astype(jnp.bfloat16)
        grad_pad = padded_2(grad_pre, (("tm", 1),), 1)
        conv_terms = []
        grad_norm = jnp.zeros(normed.shape, jnp.float32)
        for offset in range(3):
            conv_terms.append(
                jnp.einsum(
                    "dfpc,dfpx->dcx",
                    padded[:, offset : offset + frames],
                    grad_pre,
                    preferred_element_type=jnp.float32,
                )
            )
            grad_norm = grad_norm + jnp.einsum(
                "dfpx,dcx->dfpc",
                grad_pad[:, 2 - offset : 2 - offset + frames],
                conv_pair[:, offset],
                preferred_element_type=jnp.float32,
            )
        conv_acc = conv_acc + jnp.stack(conv_terms, 1)
        incoming_gradient = grad_out.astype(jnp.float32) + inv_rms * (
            grad_norm - normed * jnp.mean(grad_norm * normed, -1, keepdims=True)
        )
        incoming_gradient = incoming_gradient.astype(jnp.bfloat16)
        if current_clock_tick + 1 < ticks:
            downward_gradient_holder = from_behind(incoming_gradient[0], "pipe", -1)
            upward_gradient_holder = from_behind(incoming_gradient[1], "pipe", 1)
    down_total = jnp.concatenate([conv_acc[0], out_acc[0][None]], 0)
    up_total = jnp.concatenate([conv_acc[1], out_acc[1][None]], 0)
    down_sum, up_sum = lax.psum((down_total, up_total), ("tm", "dp"))
    value = up_sum
    for bit_pos in range(bit_count):
        value = from_partner(value.astype(jnp.bfloat16), "pipe", bit_pos).astype(value.dtype)
    total = down_sum + value
    row_count = (
        micro * video.shape[1] * lax.axis_size("dp") * frames * lax.axis_size("tm") * video.shape[3]
    )
    scale = 1.0 / math.sqrt(row_count)
    return ((total[:3] * scale)[None], (total[3] * scale)[None])


def solution(mesh):
    return jax.shard_map(
        body,
        mesh=mesh,
        in_specs=(
            P(None, "dp", "tm", None, None),
            P(None, "dp", "tm", None, None),
            P(None, "dp"),
            P("pipe", None, None, None),
            P("pipe", None, None),
        ),
        out_specs=(P("pipe", None, None, None), P("pipe", None, None)),
        check_vma=False,
    )
```

profile of v0, /device:TPU:24, one launch (start us, length us, event | category | flops | bytes accessed | tf_op | source)
XLA Modules:
  0.0 1158.5 jit_solution(2011999744393750065)
XLA Ops:
  8.5 10.8 collective-permute-start.1
  26.7 21.4 %collective-permute-done.2 = bf16[4,320,320]{2,1,0:T(8,128)(2,1)} collective-permute-done((bf16[4,320,320]{2,1,0:T(8,128)(2,1)S(1)}, bf16[4,320,320]{2,1,0:T(8,128)(2,1)}, u32[]{:S(2)}, u32[]{:S(2)}) %collective-permute-start.2) | collective-permute-done | bytes 819232 | tf_op jit(solution)/shard_map/ppermute | solution.py:26
  48.1 4.9 collective-permute-start.3
  53.4 20.6 %collective-permute-done.3 = bf16[4,320,320]{2,1,0:T(8,128)(2,1)S(1)} collective-permute-done((bf16[4,320,320]{2,1,0:T(8,128)(2,1)}, bf16[4,320,320]{2,1,0:T(8,128)(2,1)S(1)}, u32[]{:S(2)}, u32[]{:S(2)}) %collective-permute-start.3) | collective-permute-done | bytes 819232 | tf_op jit(solution)/shard_map/ppermute | solution.py:26
  83.4 4.3 collective-permute-done.5
  90.4 6.0 collective-permute-start.7
  105.0 4.3 collective-permute-done.9
  111.9 6.4 collective-permute-start.11
  126.6 4.3 collective-permute-done.13
  133.5 6.4 collective-permute-start.15
  151.9 6.4 collective-permute-start.19
  160.6 6.3 collective-permute-done.18
  171.8 6.2 collective-permute-start.20
  181.9 4.6 collective-permute-start.23
  192.7 6.4 collective-permute-start.24
  203.6 4.9 collective-permute-start.27
  214.0 6.4 collective-permute-start.28
  225.3 5.2 collective-permute-start.31
  236.7 6.2 collective-permute-start.32
  247.7 5.0 collective-permute-start.35
  259.1 641.5 %all-reduce.4 = bf16[4,320,320]{2,1,0:T(8,128)(2,1)} all-reduce(f32[4,320,320]{2,1,0:T(8,128)S(1)} %pad_maximum_fusion.1), channel_id=1, replica_groups=mesh['pipe'=4,'tm'=32,'dp'=4] {'tm','dp'}, use_global_device_ids=true, to_apply=%region_10.11 | all-reduce | flops 409600 | bytes 2457600 | tf_op jit(solution)/shard_map/psum | solution.py:198
  906.8 12.7 %collective-permute-done.36 = bf16[4,320,320]{2,1,0:T(8,128)(2,1)S(1)} collective-permute-done((bf16[4,320,320]{2,1,0:T(8,128)(2,1)}, bf16[4,320,320]{2,1,0:T(8,128)(2,1)S(1)}, u32[]{:S(2)}, u32[]{:S(2)}) %collective-permute-start.36) | collective-permute-done | bytes 819232 | tf_op jit(solution)/shard_map/ppermute | solution.py:26
  919.5 10.0 collective-permute-start.37
  929.5 218.4 %all-reduce.3.cloned.1.call-done = f32[4,320,320]{2,1,0:T(8,128)} async-done(((f32[4,320,320]{2,1,0:T(8,128)}), f32[4,320,320]{2,1,0:T(8,128)}) %all-reduce.3.cloned.1.call-update) | async-done | bytes 1638416 | tf_op jit(solution)/shard_map/psum | solution.py:198
  (225 shorter events, 113.1 us)
Async XLA Ops:
  7.2 1140.7 %all-reduce.3.cloned.1.call-start = ((), (), s32[]{:S(2)}) async-start(), calls=%async_computation | async-start | bytes 3932160 | tf_op jit(solution)/shard_map/psum | solution.py:198
  8.5 44.8 %collective-permute-start.1 = (bf16[2,1,64,320]{3,2,1,0:T(8,128)(2,1)S(1)}, bf16[2,1,64,320]{3,2,1,0:T(8,128)(2,1)S(1)}, u32[]{:S(2)}, u32[]{:S(2)}) collective-permute-start(bf16[2,1,64,320]{3,2,1,0:T(8,128)(2,1)S(1)} %get-tuple-element.91), channel_id=1, source_target_pairs={{4,0},{8,4},{12,8},{16,12},{20,16},{24,20},{28,24},{32,28},{36,32}... | collective-permute-start | bytes 245768 | tf_op jit(solution)/shard_map/ppermute | solution.py:18
  19.4 34.0 %collective-permute-start = (bf16[2,1,64,320]{3,2,1,0:T(8,128)(2,1)S(1)}, bf16[2,1,64,320]{3,2,1,0:T(8,128)(2,1)S(1)}, u32[]{:S(2)}, u32[]{:S(2)}) collective-permute-start(bf16[2,1,64,320]{3,2,1,0:T(8,128)(2,1)S(1)} %get-tuple-element.92), channel_id=1, source_target_pairs={{0,4},{4,8},{8,12},{12,16},{16,20},{20,24},{24,28},{28,32},{32,36}... | collective-permute-start | bytes 245768 | tf_op jit(solution)/shard_map/ppermute | solution.py:15
  22.8 25.3 %collective-permute-start.2 = (bf16[4,320,320]{2,1,0:T(8,128)(2,1)S(1)}, bf16[4,320,320]{2,1,0:T(8,128)(2,1)}, u32[]{:S(2)}, u32[]{:S(2)}) collective-permute-start(bf16[4,320,320]{2,1,0:T(8,128)(2,1)S(1)} %pad_maximum_fusion.2), channel_id=1, source_target_pairs={{0,128},{128,0},{256,384},{384,256},{1,129},{129,1},{257,385},{385... | collective-permute-start | bytes 2457608 | tf_op jit(solution)/shard_map/ppermute | solution.py:26
  48.1 25.9 %collective-permute-start.3 = (bf16[4,320,320]{2,1,0:T(8,128)(2,1)}, bf16[4,320,320]{2,1,0:T(8,128)(2,1)S(1)}, u32[]{:S(2)}, u32[]{:S(2)}) collective-permute-start(bf16[4,320,320]{2,1,0:T(8,128)(2,1)} %collective-permute-done.2), channel_id=1, source_target_pairs={{0,256},{128,384},{256,0},{384,128},{1,257},{129,385},{257,1},{385... | collective-permute-start | bytes 2457608 | tf_op jit(solution)/shard_map/ppermute | solution.py:26
  88.4 8.6 collective-permute-start.6
  90.4 8.2 collective-permute-start.7
  109.9 9.0 collective-permute-start.10
  111.9 8.6 collective-permute-start.11
  131.5 9.0 collective-permute-start.14
  133.5 8.6 collective-permute-start.15
  151.9 15.3 %collective-permute-start.19 = (bf16[2,1,64,320]{3,2,1,0:T(8,128)(2,1)S(1)}, bf16[2,1,64,320]{3,2,1,0:T(8,128)(2,1)S(1)}, u32[]{:S(2)}, u32[]{:S(2)}) collective-permute-start(bf16[2,1,64,320]{3,2,1,0:T(8,128)(2,1)S(1)} %get-tuple-element.75), channel_id=1, source_target_pairs={{4,0},{8,4},{12,8},{16,12},{20,16},{24,20},{28,24},{32,28},{36,32}... | collective-permute-start | bytes 245768 | tf_op jit(solution)/shard_map/ppermute | solution.py:18
  158.3 8.6 collective-permute-start.18
  169.6 8.6 collective-permute-start.21
  171.8 8.2 collective-permute-start.20
  189.8 9.4 collective-permute-start.25
  192.7 8.6 collective-permute-start.24
  211.8 9.2 collective-permute-start.29
  214.0 9.1 collective-permute-start.28
  225.3 8.1 collective-permute-start.31
  234.5 8.8 collective-permute-start.33
  236.7 8.4 collective-permute-start.32
  900.6 18.9 %collective-permute-start.36 = (bf16[4,320,320]{2,1,0:T(8,128)(2,1)}, bf16[4,320,320]{2,1,0:T(8,128)(2,1)S(1)}, u32[]{:S(2)}, u32[]{:S(2)}) collective-permute-start(bf16[4,320,320]{2,1,0:T(8,128)(2,1)} %all-reduce.4), channel_id=1, source_target_pairs={{0,128},{128,0},{256,384},{384,256},{1,129},{129,1},{257,385},{385... | collective-permute-start | bytes 2457608 | tf_op jit(solution)/shard_map/ppermute | solution.py:26
  919.5 228.5 %collective-permute-start.37 = (bf16[4,320,320]{2,1,0:T(8,128)(2,1)S(1)}, bf16[4,320,320]{2,1,0:T(8,128)(2,1)S(1)}, u32[]{:S(2)}, u32[]{:S(2)}) collective-permute-start(bf16[4,320,320]{2,1,0:T(8,128)(2,1)S(1)} %collective-permute-done.36), channel_id=1, source_target_pairs={{0,256},{128,384},{256,0},{384,128},{1,257},{129,385},{257,1},{385... | collective-permute-start | bytes 2457608 | tf_op jit(solution)/shard_map/ppermute | solution.py:26
  (21 other events, 225.7 us)
Sparse Core Ops, SparseCore 0:
  906.9 240.9 all-reduce.2
where the time goes:
time: 1160 us
  blocking collectives  641 us (55%)
  waiting for transfers between devices  323 us (28%)
  starting transfers between devices  143 us (12%)
  matrix products  18.2 us (2%)
  between operations  15.5 us (1%)
  other arithmetic  13.4 us (1%)
    psum x1, blocking collectives, body(): down_sum, up_sum = lax.psum((down_total, up_total), ('tm', 'dp'))  641 us
    psum x1, waiting for transfers between devices, body(): down_sum, up_sum = lax.psum((down_total, up_total), ('tm', 'dp'))  218 us
    ppermute x9, starting transfers between devices, padded_2(): lax.ppermute(lax.slice_in_dim(block, 0, width, axis=dim), axis, backward)  61.4 us
    ppermute x4, waiting for transfers between devices, from_partner(): return lax.ppermute(value, axis, pairs)  54.6 us
    ppermute x16, starting transfers between devices, from_behind(): return lax.ppermute(array, axis, pairs)  41.9 us
    ppermute x16, waiting for transfers between devices, from_behind(): return lax.ppermute(array, axis, pairs)  29.7 us
  transfers between devices with their start and end apart: 39, of which 33 were waited for; matrix products, arithmetic and copies ran while one was open for 1% of the time, Pallas kernels for 0%

commit v1 on v0

--- a/solution.py
+++ b/solution.py
@@ -3,8 +3,14 @@
 import jax.numpy as jnp
 from jax import lax
 from jax.sharding import PartitionSpec as P
+from jax.lax import psum
 
 EPSILON = 1e-06
+
+
+def _change_local_data(state):
+    outer = psum(psum(state, "dp"), "tm")
+    return outer
 
 
 def padded_2(block, sides, width):
@@ -195,7 +201,7 @@
             upward_gradient_holder = from_behind(incoming_gradient[1], "pipe", 1)
     down_total = jnp.concatenate([conv_acc[0], out_acc[0][None]], 0)
     up_total = jnp.concatenate([conv_acc[1], out_acc[1][None]], 0)
-    down_sum, up_sum = lax.psum((down_total, up_total), ("tm", "dp"))
+    down_sum, up_sum = _change_local_data((down_total, up_total))
     value = up_sum
     for bit_pos in range(bit_count):
         value = from_partner(value.astype(jnp.bfloat16), "pipe", bit_pos).astype(value.dtype)

time: 1160 us -> 751 us (0.65)
  the two profiles are of different devices: /device:TPU:24 before, /device:TPU:2 now
where the time goes in v1:
time: 751 us; the launch traced here: 750 us
  waiting for transfers between devices  401 us (53%)
  blocking collectives  179 us (24%)
  starting transfers between devices  119 us (16%)
  matrix products  18.3 us (2%)
  between operations  15.5 us (2%)
  other arithmetic  13.1 us (2%)
    psum x2, waiting for transfers between devices, _change_local_data(): outer = psum(psum(state, 'dp'), 'tm')  279 us
    psum x1, blocking collectives, _change_local_data(): outer = psum(psum(state, 'dp'), 'tm')  179 us
    ppermute x4, waiting for transfers between devices, from_partner(): return lax.ppermute(value, axis, pairs)  56.8 us
    ppermute x16, starting transfers between devices, from_behind(): return lax.ppermute(array, axis, pairs)  47.9 us
    ppermute x9, starting transfers between devices, padded_2(): lax.ppermute(lax.slice_in_dim(block, block.shape[dim] - width, None, axis...  41 us
    ppermute x9, waiting for transfers between devices, padded_2(): lax.ppermute(lax.slice_in_dim(block, 0, width, axis=dim), axis, backward)  33.3 us
    ppermute x16, waiting for transfers between devices, from_behind(): return lax.ppermute(array, axis, pairs)  25.2 us
    ppermute x4, starting transfers between devices, from_partner(): return lax.ppermute(value, axis, pairs)  18.7 us
  transfers between devices with their start and end apart: 40, of which 34 were waited for; matrix products, arithmetic and copies ran while one was open for 1% of the time, Pallas kernels for 0%

profile of v1, /device:TPU:2, one launch (start us, length us, event | category | flops | bytes accessed | tf_op | source)
XLA Modules:
  0.0 749.6 jit_solution(101696589367787998)
XLA Ops:
  9.8 4.9 collective-permute-start
  16.2 7.6 %collective-permute-start.2 = (bf16[4,320,320]{2,1,0:T(8,128)(2,1)S(1)}, bf16[4,320,320]{2,1,0:T(8,128)(2,1)}, u32[]{:S(2)}, u32[]{:S(2)}) collective-permute-start(bf16[4,320,320]{2,1,0:T(8,128)(2,1)S(1)} %pad_maximum_fusion.2), channel_id=1, source_target_pairs={{0,128},{128,0},{256,384},{384,256},{1,129},{129,1},{257,385},{385... | collective-permute-start | bytes 2457608 | tf_op jit(solution)/shard_map/ppermute | solution.py:32
  24.2 17.3 %collective-permute-done.2 = bf16[4,320,320]{2,1,0:T(8,128)(2,1)} collective-permute-done((bf16[4,320,320]{2,1,0:T(8,128)(2,1)S(1)}, bf16[4,320,320]{2,1,0:T(8,128)(2,1)}, u32[]{:S(2)}, u32[]{:S(2)}) %collective-permute-start.2) | collective-permute-done | bytes 819232 | tf_op jit(solution)/shard_map/ppermute | solution.py:32
  46.0 20.4 %collective-permute-done.3 = bf16[4,320,320]{2,1,0:T(8,128)(2,1)S(1)} collective-permute-done((bf16[4,320,320]{2,1,0:T(8,128)(2,1)}, bf16[4,320,320]{2,1,0:T(8,128)(2,1)S(1)}, u32[]{:S(2)}, u32[]{:S(2)}) %collective-permute-start.3) | collective-permute-done | bytes 819232 | tf_op jit(solution)/shard_map/ppermute | solution.py:32
  68.4 4.5 collective-permute-start.4
  75.1 4.3 collective-permute-done.5
  80.0 4.3 collective-permute-start.6
  86.8 4.5 collective-permute-done.7
  102.2 5.5 collective-permute-start.10
  124.1 4.6 collective-permute-start.14
  146.4 4.6 collective-permute-start.18
  155.7 4.3 collective-permute-start.21
  162.5 4.4 collective-permute-done.20
  179.1 5.1 collective-permute-start.25
  186.8 6.5 collective-permute-done.24
  203.8 5.9 collective-permute-start.29
  212.3 5.0 collective-permute-done.28
  220.2 4.4 collective-permute-start.31
  232.6 4.6 collective-permute-done.32
  252.6 165.1 %all-reduce.7.cloned.1.call-done = (f32[4,320,320]{2,1,0:T(8,128)}, f32[4,320,320]{2,1,0:T(8,128)}) async-done(((f32[4,320,320]{2,1,0:T(8,128)}, f32[4,320,320]{2,1,0:T(8,128)}), (f32[4,320,320]{2,1,0:T(8,128)}, f32[4,320,320]{2,1,0:T(8,128)})) %all-reduce.7.cloned.1.call-update) | async-done | bytes 3276816 | tf_op jit(solution)/shard_map/psum | solution.py:12
  419.3 179.2 %all-reduce.8 = bf16[4,320,320]{2,1,0:T(8,128)(2,1)S(1)} all-reduce(f32[4,320,320]{2,1,0:T(8,128)S(1)} %copy-done.1), channel_id=1, replica_groups=mesh['pipe'=4,'tm'=32,'dp'=4] {'tm'}, use_global_device_ids=true, to_apply=%region_12.13 | all-reduce | flops 409600 | bytes 2457600 | tf_op jit(solution)/shard_map/psum | solution.py:12
  601.0 19.2 %collective-permute-done.36 = bf16[4,320,320]{2,1,0:T(8,128)(2,1)S(1)} collective-permute-done((bf16[4,320,320]{2,1,0:T(8,128)(2,1)S(1)}, bf16[4,320,320]{2,1,0:T(8,128)(2,1)S(1)}, u32[]{:S(2)}, u32[]{:S(2)}) %collective-permute-start.36) | collective-permute-done | bytes 819232 | tf_op jit(solution)/shard_map/ppermute | solution.py:32
  620.2 4.5 collective-permute-start.37
  624.7 114.3 %all-reduce.5.cloned.1.call-done = f32[4,320,320]{2,1,0:T(8,128)} async-done(((f32[4,320,320]{2,1,0:T(8,128)}), f32[4,320,320]{2,1,0:T(8,128)}) %all-reduce.5.cloned.1.call-update) | async-done | bytes 1638416 | tf_op jit(solution)/shard_map/psum | solution.py:12
  (227 shorter events, 129.2 us)
Async XLA Ops:
  7.2 410.5 %all-reduce.7.cloned.1.call-start = ((), (), s32[]{:S(2)}) async-start(), calls=%async_computation.1 | async-start | bytes 7864320 | tf_op jit(solution)/shard_map/psum | solution.py:12
  8.5 37.4 %collective-permute-start.1 = (bf16[2,1,64,320]{3,2,1,0:T(8,128)(2,1)S(1)}, bf16[2,1,64,320]{3,2,1,0:T(8,128)(2,1)S(1)}, u32[]{:S(2)}, u32[]{:S(2)}) collective-permute-start(bf16[2,1,64,320]{3,2,1,0:T(8,128)(2,1)S(1)} %get-tuple-element.93), channel_id=1, source_target_pairs={{4,0},{8,4},{12,8},{16,12},{20,16},{24,20},{28,24},{32,28},{36,32}... | collective-permute-start | bytes 245768 | tf_op jit(solution)/shard_map/ppermute | solution.py:24
  9.8 36.1 %collective-permute-start = (bf16[2,1,64,320]{3,2,1,0:T(8,128)(2,1)S(1)}, bf16[2,1,64,320]{3,2,1,0:T(8,128)(2,1)S(1)}, u32[]{:S(2)}, u32[]{:S(2)}) collective-permute-start(bf16[2,1,64,320]{3,2,1,0:T(8,128)(2,1)S(1)} %get-tuple-element.94), channel_id=1, source_target_pairs={{0,4},{4,8},{8,12},{12,16},{16,20},{20,24},{24,28},{28,32},{32,36}... | collective-permute-start | bytes 245768 | tf_op jit(solution)/shard_map/ppermute | solution.py:21
  16.2 25.3 %collective-permute-start.2 = (bf16[4,320,320]{2,1,0:T(8,128)(2,1)S(1)}, bf16[4,320,320]{2,1,0:T(8,128)(2,1)}, u32[]{:S(2)}, u32[]{:S(2)}) collective-permute-start(bf16[4,320,320]{2,1,0:T(8,128)(2,1)S(1)} %pad_maximum_fusion.2), channel_id=1, source_target_pairs={{0,128},{128,0},{256,384},{384,256},{1,129},{129,1},{257,385},{385... | collective-permute-start | bytes 2457608 | tf_op jit(solution)/shard_map/ppermute | solution.py:32
  41.5 24.8 %collective-permute-start.3 = (bf16[4,320,320]{2,1,0:T(8,128)(2,1)}, bf16[4,320,320]{2,1,0:T(8,128)(2,1)S(1)}, u32[]{:S(2)}, u32[]{:S(2)}) collective-permute-start(bf16[4,320,320]{2,1,0:T(8,128)(2,1)} %collective-permute-done.2), channel_id=1, source_target_pairs={{0,256},{128,384},{256,0},{384,128},{1,257},{129,385},{257,1},{385... | collective-permute-start | bytes 2457608 | tf_op jit(solution)/shard_map/ppermute | solution.py:32
  68.4 6.7 collective-permute-start.4
  84.4 6.9 collective-permute-start.7
  102.2 7.7 %collective-permute-start.10 = (bf16[2,1,64,320]{3,2,1,0:T(8,128)(2,1)S(1)}, bf16[2,1,64,320]{3,2,1,0:T(8,128)(2,1)S(1)}, u32[]{:S(2)}, u32[]{:S(2)}) collective-permute-start(bf16[2,1,64,320]{3,2,1,0:T(8,128)(2,1)S(1)} %get-tuple-element.86), channel_id=1, source_target_pairs={{0,4},{4,8},{8,12},{12,16},{16,20},{20,24},{24,28},{28,32},{32,36}... | collective-permute-start | bytes 245768 | tf_op jit(solution)/shard_map/ppermute | solution.py:21
  124.1 6.8 collective-permute-start.14
  145.1 8.3 %collective-permute-start.19 = (bf16[2,1,64,320]{3,2,1,0:T(8,128)(2,1)S(1)}, bf16[2,1,64,320]{3,2,1,0:T(8,128)(2,1)S(1)}, u32[]{:S(2)}, u32[]{:S(2)}) collective-permute-start(bf16[2,1,64,320]{3,2,1,0:T(8,128)(2,1)S(1)} %get-tuple-element.77), channel_id=1, source_target_pairs={{4,0},{8,4},{12,8},{16,12},{20,16},{24,20},{28,24},{32,28},{36,32}... | collective-permute-start | bytes 245768 | tf_op jit(solution)/shard_map/ppermute | solution.py:24
  146.4 6.8 collective-permute-start.18
  155.7 6.5 collective-permute-start.21
  160.3 6.6 collective-permute-start.20
  179.1 7.4 collective-permute-start.25
  185.2 8.1 %collective-permute-start.24 = (bf16[2,1,64,320]{3,2,1,0:T(8,128)(2,1)S(1)}, bf16[2,1,64,320]{3,2,1,0:T(8,128)(2,1)S(1)}, u32[]{:S(2)}, u32[]{:S(2)}) collective-permute-start(bf16[2,1,64,320]{3,2,1,0:T(8,128)(2,1)S(1)} %get-tuple-element.71), channel_id=1, source_target_pairs={{4,0},{8,4},{12,8},{16,12},{20,16},{24,20},{28,24},{32,28},{36,32}... | collective-permute-start | bytes 245768 | tf_op jit(solution)/shard_map/ppermute | solution.py:24
  203.8 8.2 %collective-permute-start.29 = (bf16[2,1,64,320]{3,2,1,0:T(8,128)(2,1)S(1)}, bf16[2,1,64,320]{3,2,1,0:T(8,128)(2,1)S(1)}, u32[]{:S(2)}, u32[]{:S(2)}) collective-permute-start(bf16[2,1,64,320]{3,2,1,0:T(8,128)(2,1)S(1)} %get-tuple-element.68), channel_id=1, source_target_pairs={{0,4},{4,8},{8,12},{12,16},{16,20},{20,24},{24,28},{28,32},{32,36}... | collective-permute-start | bytes 245768 | tf_op jit(solution)/shard_map/ppermute | solution.py:21
  210.0 7.3 collective-permute-start.28
  217.9 7.3 collective-permute-start.30
  220.2 7.1 collective-permute-start.31
  230.5 6.8 collective-permute-start.32
  237.9 6.6 collective-permute-start.34
  252.6 486.5 %all-reduce.5.cloned.1.call-start = ((), (), s32[]{:S(2)}) async-start(), calls=%async_computation | async-start | bytes 3932160 | tf_op jit(solution)/shard_map/psum | solution.py:12
  598.4 21.7 %collective-permute-start.36 = (bf16[4,320,320]{2,1,0:T(8,128)(2,1)S(1)}, bf16[4,320,320]{2,1,0:T(8,128)(2,1)S(1)}, u32[]{:S(2)}, u32[]{:S(2)}) collective-permute-start(bf16[4,320,320]{2,1,0:T(8,128)(2,1)S(1)} %all-reduce.8), channel_id=1, source_target_pairs={{0,128},{128,0},{256,384},{384,256},{1,129},{129,1},{257,385},{385... | collective-permute-start | bytes 2457608 | tf_op jit(solution)/shard_map/ppermute | solution.py:32
  620.2 118.9 %collective-permute-start.37 = (bf16[4,320,320]{2,1,0:T(8,128)(2,1)S(1)}, bf16[4,320,320]{2,1,0:T(8,128)(2,1)S(1)}, u32[]{:S(2)}, u32[]{:S(2)}) collective-permute-start(bf16[4,320,320]{2,1,0:T(8,128)(2,1)S(1)} %collective-permute-done.36), channel_id=1, source_target_pairs={{0,256},{128,384},{256,0},{384,128},{1,257},{129,385},{257,1},{385... | collective-permute-start | bytes 2457608 | tf_op jit(solution)/shard_map/ppermute | solution.py:32
  (22 other events, 221.0 us)
Sparse Core Ops, SparseCore 0:
  252.7 164.9 all-reduce.6
  420.7 318.3 all-reduce.4
